TPU v7x, 32 devices: a whole 2x2x4 slice. The times are simulated.
32 devices in a mesh: section: 2 (over core), seq: 16 (over z, y, x).
Axes of the slice: x: 2, y: 2, z: 4, core: 2. Of those that a mesh axis runs over, the one named last changes fastest.
Arguments:
- bases: int32 [2, 8192], P(None, 'seq'), may hold values from 0 to 3
- stem_weight: bfloat16 [15, 4, 1536], replicated, may hold values from -1.5 to 1.5
- gains: bfloat16 [2, 1536], P('section'), may hold values from 0.099609375 to 1.8984375
- depth_taps: bfloat16 [2, 5, 1536], P('section'), may hold values from -2.5 to 2.5
- point_weight: bfloat16 [2, 1536, 1536], P('section', 'seq'), may hold values from -0.15625 to 0.15625
Outputs:
- encoded: bfloat16 [2, 2048, 1536], P(None, 'seq', 'section')
All inputs are finite; a program needn't handle non-finite values.
Results may differ from a plain program's by a relative error of at most 0.015.
Values may be sent and summed in bfloat16 or wider, within the bound.
A program may use at most 64 MiB of HBM per device.

v0:
```python
import jax
import jax.numpy as jnp
from jax import lax
from jax.sharding import PartitionSpec as P

DILATION_STEP = 2


def padded(array, sides, width):
    for axis, dim in sides:
        size, length = (lax.axis_size(axis), array.shape[dim])
        up = [(i, (i + 1) % size) for i in range(size - 1)]
        down = [(j, i) for i, j in up]
        last = lax.slice_in_dim(array, length - width, length, axis=dim)
        first = lax.slice_in_dim(array, 0, width, axis=dim)
        before = lax.ppermute(last, axis, up)
        after = lax.ppermute(first, axis, down)
        array = jnp.concatenate([before, array, after], axis=dim)
    return array


def shortened(array):

    def short(part):
        return part.astype(jnp.bfloat16) if part.dtype == jnp.float32 else part

    return jax.tree.map(short, array)


def passed_along(array, axis, by):
    length = lax.axis_size(axis)
    pairs = [(i, i + by) for i in range(length) if 0 <= i + by < length]
    return lax.ppermute(array, axis, pairs)


def from_root(value, axis, source):
    kept = jnp.where(lax.axis_index(axis) == source, value, 0).astype(value.dtype)
    return lax.psum(kept, axis)


def normalize_gelu(rows, gain_row):
    values = rows.astype(jnp.float32)
    square_mean = jnp.mean(values * values, axis=-1, keepdims=True)
    scaled = values * lax.rsqrt(square_mean + 1e-06) * gain_row.astype(jnp.float32)
    return jax.nn.gelu(scaled, approximate=True).astype(jnp.bfloat16)


def filter_rows(extended_rows, kernel_weight, length_total):
    summed = jnp.zeros((length_total, extended_rows.shape[1]), jnp.float32)
    for offset_amount in range(kernel_weight.shape[0]):
        window_rows = extended_rows[
            offset_amount * DILATION_STEP : offset_amount * DILATION_STEP + length_total
        ].astype(jnp.float32)
        summed = summed + kernel_weight[offset_amount].astype(jnp.float32) * window_rows
    return summed.astype(jnp.bfloat16)


def halve_rows(rows):
    return jnp.max(rows.reshape(rows.shape[0] // 2, 2, rows.shape[1]), axis=1)


def stem_rows(extended_ids, stem_weight, length_total):
    one_hot = (extended_ids[:, None] == jnp.arange(1, 5, dtype=jnp.int32)[None, :]).astype(
        jnp.bfloat16
    )
    window_rows = jnp.concatenate(
        [
            one_hot[offset_amount : offset_amount + length_total]
            for offset_amount in range(stem_weight.shape[0])
        ],
        axis=1,
    )
    flat = stem_weight.reshape(stem_weight.shape[0] * 4, stem_weight.shape[2])
    return jnp.dot(window_rows, flat, preferred_element_type=jnp.float32).astype(jnp.bfloat16)


def shards(bases, stem_weight, gains, depth_taps, point_weight):
    section_count = lax.axis_size("section")
    position = lax.axis_index("section")
    sequences, width_rows = bases.shape
    channels = stem_weight.shape[2]
    margin = stem_weight.shape[0] // 2
    padded_ids = padded(bases + 1, (("seq", 1),), margin)
    stems = jnp.stack(
        [stem_rows(padded_ids[index], stem_weight, width_rows) for index in range(sequences)]
    )
    gain_row = gains[0]
    kernel_weight = depth_taps[0]
    spread_width = kernel_weight.shape[0] // 2 * DILATION_STEP
    half_rows = width_rows // 2
    final_rows = width_rows >> section_count
    steps_total = sequences + section_count - 1
    first_section = position == 0
    valid_count = jnp.right_shift(jnp.int32(width_rows), position)

    def edge_rims(stem_now, inbox):
        head = jnp.where(first_section, stem_now[:spread_width], inbox[:spread_width])
        inbox_tail = lax.dynamic_slice_in_dim(inbox, valid_count - spread_width, spread_width, 0)
        tail = jnp.where(first_section, stem_now[width_rows - spread_width :], inbox_tail)
        edges = jnp.concatenate([head, tail], axis=0)
        framed = padded(normalize_gelu(edges, gain_row), (("seq", 0),), spread_width)
        return (framed[:spread_width], framed[3 * spread_width :])

    def prepare(level_rows, left_rim, right_rim):
        activated = normalize_gelu(level_rows, gain_row)
        extended_rows = jnp.concatenate([left_rim, activated, right_rim], axis=0)
        return filter_rows(extended_rows, kernel_weight, level_rows.shape[0])

    def complete(level_rows, product):
        pooled = halve_rows((level_rows.astype(jnp.float32) + product).astype(jnp.bfloat16))
        if pooled.shape[0] < half_rows:
            pooled = jnp.concatenate(
                [pooled, jnp.zeros((half_rows - pooled.shape[0], channels), jnp.bfloat16)], axis=0
            )
        return pooled

    def pass_on(pooled):
        return jax.tree.map(
            lambda part, own: part.astype(own.dtype),
            passed_along(shortened(pooled), "section", 1),
            pooled,
        )

    inbox_start = jnp.zeros((half_rows, channels), jnp.bfloat16)
    first_rows = stems[0]
    left_first, right_first = edge_rims(first_rows, inbox_start)
    filtered_first = prepare(first_rows, left_first, right_first)
    weights_full = lax.all_gather(point_weight, "seq", axis=1, tiled=True)[0]
    product_first = jnp.dot(filtered_first, weights_full, preferred_element_type=jnp.float32)
    inbox = pass_on(complete(first_rows, product_first))
    outbox = jnp.zeros((sequences, final_rows, channels), jnp.bfloat16)

    def make_level(level):
        count = width_rows >> level

        def run(operands):
            stem_now, inbox_now, left_rim, right_rim = operands
            level_rows = stem_now if level == 0 else inbox_now[:count]
            filtered = prepare(level_rows, left_rim, right_rim)
            product = jnp.dot(filtered, weights_full, preferred_element_type=jnp.float32)
            return complete(level_rows, product)

        return run

    branches = [make_level(level) for level in range(section_count)]

    def advance(inbox_now, outbox_now, step_index):
        micro_index = step_index - position
        live = (micro_index >= 0) & (micro_index < sequences)
        clipped = jnp.clip(micro_index, 0, sequences - 1)
        stem_now = lax.dynamic_index_in_dim(stems, clipped, 0, keepdims=False)
        left_rim, right_rim = edge_rims(stem_now, inbox_now)

        def working(operands):
            return lax.switch(position, branches, operands)

        def resting(operands):
            return jnp.zeros((half_rows, channels), jnp.bfloat16)

        pooled = lax.cond(live, working, resting, (stem_now, inbox_now, left_rim, right_rim))
        keep = live & (position == section_count - 1)
        updated = lax.dynamic_update_index_in_dim(outbox_now, pooled[:final_rows], clipped, 0)
        return (pooled, jnp.where(keep, updated, outbox_now))

    def middle_step(carry, step_index):
        pooled, outbox_next = advance(carry[0], carry[1], step_index)
        return ((pass_on(pooled), outbox_next), None)

    (inbox, outbox), unused = lax.scan(
        middle_step, (inbox, outbox), jnp.arange(1, steps_total - 1, dtype=jnp.int32)
    )
    pooled_last, outbox = advance(inbox, outbox, jnp.int32(steps_total - 1))
    coarsest = from_root(outbox, "section", section_count - 1)
    out_width = channels // section_count
    return lax.dynamic_slice_in_dim(coarsest, position * out_width, out_width, 2)


def solution(mesh):
    return jax.shard_map(
        shards,
        mesh=mesh,
        in_specs=(
            P(None, "seq"),
            P(),
            P("section", None),
            P("section", None, None),
            P("section", "seq", None),
        ),
        out_specs=P(None, "seq", "section"),
        check_vma=False,
    )
```

profile of v0, /device:TPU:0, one launch (start us, length us, event | category | flops | bytes accessed | tf_op | source)
XLA Modules:
  0.0 200.0 jit_solution(13263044723846693947)
XLA Ops:
  8.1 4.8 %collective-permute-start = (s32[2,7]{1,0:T(2,128)S(1)}, s32[2,7]{1,0:T(2,128)S(1)}, u32[]{:S(2)}, u32[]{:S(2)}) collective-permute-start(s32[2,7]{1,0:T(2,128)S(1)} %get-tuple-element.250), channel_id=1, source_target_pairs={{0,1},{1,2},{2,3},{3,4},{4,5},{5,6},{6,7},{7,8},{8,9},{9,10},{10,1... | collective-permute-start | bytes 176 | tf_op jit(solution)/shard_map/ppermute | solution.py:16
  15.9 1.6 convert_reduce_fusion.24
  20.8 4.4 %collective-permute-start.2 = (bf16[4,1536]{1,0:T(4,128)(2,1)S(1)}, bf16[4,1536]{1,0:T(4,128)(2,1)S(1)}, u32[]{:S(2)}, u32[]{:S(2)}) collective-permute-start(bf16[4,1536]{1,0:T(4,128)(2,1)S(1)} %get-tuple-element.248), channel_id=1, source_target_pairs={{0,1},{1,2},{2,3},{3,4},{4,5},{5,6},{6,7},{7,8},{8,9},{9,10},{10,1... | collective-permute-start | bytes 36872 | tf_op jit(solution)/shard_map/ppermute | solution.py:16
  25.3 1.9 collective-permute-start.3
  27.2 2.5 %fusion.88 = bf16[512,1536]{1,0:T(8,128)(2,1)} fusion(bf16[512,1536]{1,0:T(8,128)(2,1)S(1)} %get-tuple-element.255, f32[1536]{0:T(1024)S(1)} %mul.567, f32[512]{0:T(512)S(1)} %add_rsqrt_fusion.4), kind=kLoop, calls=%fused_computation.166 | loop fusion | flops 9437184 | bytes 3153920 | tf_op jit(solution)/shard_map/convert_element_type | solution.py:45
  30.9 62.5 %all-gather.2.cloned.1.call-done = bf16[1,1536,1536]{2,1,0:T(8,128)(2,1)} async-done(((bf16[1,96,1536]{2,1,0:T(8,128)(2,1)}), bf16[1,1536,1536]{2,1,0:T(8,128)(2,1)}) %all-gather.2.cloned.1.call-update) | async-done | bytes 4718608 | tf_op jit(solution)/shard_map/all_gather | solution.py:128
  93.4 9.7 %fusion.94 = bf16[512,1536]{1,0:T(8,128)(2,1)S(1)} fusion(bf16[512,1536]{1,0:T(8,128)(2,1)S(1)} %get-tuple-element.255, bf16[512,1536]{1,0:T(8,128)(2,1)} %fusion.88, bf16[4,1536]{1,0:T(4,128)(2,1)} %copy-done.11, bf16[4,1536]{1,0:T(4,128)(2,1)} %copy-done.10, f32[1536]{0:T(1024)S(1)} %copy-done.7, f32[1536]{0:T(1024)} %get-tuple-element.203, ...), kind=kOutput, calls=%fused_computation.173 | convolution fusion | flops 2439512064 | bytes 9492480 | tf_op jit(solution)/shard_map/dot_general | solution.py:129
  103.7 5.4 %reduce_max.45 = bf16[256,1536]{1,0:T(8,128)(2,1)} reduce(bf16[256,2,1536]{2,1,0:T(2,128)(2,1)S(1)} %reshape.147, bf16[]{:T(256)} %constant.176.clone.1), dimensions={1}, to_apply=%region_2.3 | reduce | flops 393216 | bytes 2359298 | tf_op jit(solution)/shard_map/reduce_max | solution.py:59
  109.1 2.3 %collective-permute-start.4 = (bf16[256,1536]{1,0:T(8,128)(2,1)}, bf16[256,1536]{1,0:T(8,128)(2,1)}, u32[]{:S(2)}, u32[]{:S(2)}) collective-permute-start(bf16[256,1536]{1,0:T(8,128)(2,1)} %reduce_max.45), channel_id=1, source_target_pairs={{0,16},{1,17},{2,18},{3,19},{4,20},{5,21},{6,22},{7,23},{8,24},{9,... | collective-permute-start | bytes 2359304 | tf_op jit(solution)/shard_map/ppermute | solution.py:33
  116.3 3.4 %collective-permute-start.5 = (bf16[4,1536]{1,0:T(4,128)(2,1)S(1)}, bf16[4,1536]{1,0:T(4,128)(2,1)S(1)}, u32[]{:S(2)}, u32[]{:S(2)}) collective-permute-start(bf16[4,1536]{1,0:T(4,128)(2,1)S(1)} %get-tuple-element.247), channel_id=1, source_target_pairs={{0,1},{1,2},{2,3},{3,4},{4,5},{5,6},{6,7},{7,8},{8,9},{9,10},{10,1... | collective-permute-start | bytes 36872 | tf_op jit(solution)/shard_map/while/body/eval_jaxpr/ppermute | solution.py:16
  121.0 4.2 %collective-permute-done.6 = bf16[4,1536]{1,0:T(4,128)(2,1)S(1)} collective-permute-done((bf16[4,1536]{1,0:T(4,128)(2,1)S(1)}, bf16[4,1536]{1,0:T(4,128)(2,1)S(1)}, u32[]{:S(2)}, u32[]{:S(2)}) %collective-permute-start.6) | collective-permute-done | bytes 12320 | tf_op jit(solution)/shard_map/while/body/eval_jaxpr/ppermute | solution.py:17
  125.2 18.3 %conditional.4 = (bf16[256,1536]{1,0:T(8,128)(2,1)}, bf16[1,128,1536]{2,1,0:T(8,128)(2,1)S(1)}) conditional(s32[]{:T(128)} %convert_element_type.295, () %tuple.37, (s32[]{:T(128)}, bf16[1,512,1536]{2,1,0:T(8,128)(2,1)S(1)}, bf16[5,1536]{1,0:T(8,128)(2,1)S(1)}, bf16[1536]{0:T(1024)(128)(2,1)S(1)}, bf16[4,1536]{1,0:T(4,128)(2,1)S(1)}, ...), branch_computations={%region_4.5_spmd, %region_5.12_spmd} | conditional | flops 2451711488 | bytes 39446696 | solution.py:160
  125.2 17.3 %conditional = (bf16[256,1536]{1,0:T(8,128)(2,1)}) conditional(s32[]{:T(128)} %clamp.4, (bf16[1,512,1536]{2,1,0:T(8,128)(2,1)S(1)}, bf16[5,1536]{1,0:T(8,128)(2,1)S(1)}, bf16[1536]{0:T(1024)(128)(2,1)S(1)}, bf16[4,1536]{1,0:T(4,128)(2,1)S(1)}, bf16[4,1536]{1,0:T(4,128)(2,1)S(1)}, /*index=5*/bf16[1536,1536]{1,0:T(8,128)(2,1)}) %tuple.28, ...), branch_computations={%region_6.8_spmd, %region_9.0_spmd} | conditional | flops 2451711488 | bytes 38660136 | solution.py:155
  125.6 1.4 fusion.7
  127.5 6.0 %fusion.10 = bf16[512,1536]{1,0:T(8,128)(2,1)} fusion(bf16[1536,1536]{1,0:T(8,128)(2,1)S(1)} %copy-done.8, bf16[512,1536]{1,0:T(8,128)(2,1)S(1)} %fusion.7, bf16[4,1536]{1,0:T(4,128)(2,1)S(1)} %get-tuple-element.138, bf16[4,1536]{1,0:T(4,128)(2,1)S(1)} %get-tuple-element.136, bf16[1,512,1536]{2,1,0:T(8,128)(2,1)S(1)} %get-tuple-element.134, ...), kind=kOutput, calls=%fused_computation.15 | convolution fusion | flops 2439512064 | bytes 9492480 | tf_op jit(solution)/shard_map/while/body/eval_jaxpr/cond/branch_1_fun/cond/branch_0_fun/dot_general | solution.py:140
  133.6 3.5 %reshape.140 = bf16[256,2,1536]{2,1,0:T(2,128)(2,1)S(1)} reshape(bf16[512,1536]{1,0:T(8,128)(2,1)} %fusion.10) | data formatting | bytes 3145728 | tf_op jit(solution)/shard_map/while/body/eval_jaxpr/cond/branch_1_fun/cond/branch_0_fun/reshape | solution.py:59
  137.1 5.2 %reduce_max.40 = bf16[256,1536]{1,0:T(8,128)(2,1)} reduce(bf16[256,2,1536]{2,1,0:T(2,128)(2,1)S(1)} %reshape.140, bf16[]{:T(256)} %constant.48.clone), dimensions={1}, to_apply=%region_8.7 | reduce | flops 393216 | bytes 2359298 | tf_op jit(solution)/shard_map/while/body/eval_jaxpr/cond/branch_1_fun/cond/branch_0_fun/reduce_max | solution.py:59
  143.5 1.3 collective-permute-start.7
  144.9 2.0 %collective-permute-done.7 = bf16[256,1536]{1,0:T(8,128)(2,1)S(1)} collective-permute-done((bf16[256,1536]{1,0:T(8,128)(2,1)}, bf16[256,1536]{1,0:T(8,128)(2,1)S(1)}, u32[]{:S(2)}, u32[]{:S(2)}) %collective-permute-start.7) | collective-permute-done | bytes 786464 | tf_op jit(solution)/shard_map/while/body/eval_jaxpr/ppermute | solution.py:33
  147.2 4.3 %collective-permute-start.8 = (bf16[4,1536]{1,0:T(4,128)(2,1)S(1)}, bf16[4,1536]{1,0:T(4,128)(2,1)S(1)}, u32[]{:S(2)}, u32[]{:S(2)}) collective-permute-start(bf16[4,1536]{1,0:T(4,128)(2,1)S(1)} %get-tuple-element.245), channel_id=1, source_target_pairs={{0,1},{1,2},{2,3},{3,4},{4,5},{5,6},{6,7},{7,8},{8,9},{9,10},{10,1... | collective-permute-start | bytes 36872 | tf_op jit(solution)/shard_map/ppermute | solution.py:16
  153.0 4.2 %collective-permute-done.9 = bf16[4,1536]{1,0:T(4,128)(2,1)} collective-permute-done((bf16[4,1536]{1,0:T(4,128)(2,1)S(1)}, bf16[4,1536]{1,0:T(4,128)(2,1)}, u32[]{:S(2)}, u32[]{:S(2)}) %collective-permute-start.9) | collective-permute-done | bytes 12320 | tf_op jit(solution)/shard_map/ppermute | solution.py:17
  157.2 2.0 %conditional.5 = (bf16[1,128,1536]{2,1,0:T(8,128)(2,1)}) conditional(s32[]{:T(128)} %convert_element_type.323, () %tuple.39, (s32[]{:T(128)}, bf16[1,512,1536]{2,1,0:T(8,128)(2,1)S(1)}, bf16[5,1536]{1,0:T(8,128)(2,1)}, bf16[1536]{0:T(1024)(128)(2,1)S(1)}, bf16[4,1536]{1,0:T(4,128)(2,1)S(1)}, /*index=5*/bf16[4,1536]{1,0:T(4,128)(2,1)}, ...), branch_computations={%region_13.14_spmd, %region_14.0_spmd} | conditional | flops 2451711488 | bytes 39508144 | solution.py:160
  160.4 30.7 %all-reduce.4.cloned.1.call-done = bf16[2,128,1536]{2,1,0:T(8,128)(2,1)} async-done(((bf16[2,128,1536]{2,1,0:T(8,128)(2,1)}), bf16[2,128,1536]{2,1,0:T(8,128)(2,1)}) %all-reduce.4.cloned.1.call-update) | async-done | bytes 786448 | tf_op jit(solution)/shard_map/psum | solution.py:38
  191.1 1.8 constant_dynamic-slice_fusion
  (75 shorter events, 21.2 us)
Async XLA Ops:
  6.5 86.8 %all-gather.2.cloned.1.call-start = ((), (), s32[]{:S(2)}) async-start(), calls=%async_computation | async-start | bytes 5013504 | tf_op jit(solution)/shard_map/all_gather | solution.py:128
  7.3 183.8 %all-reduce.4.cloned.1.call-start = ((), (), s32[]{:S(2)}) async-start(), calls=%async_computation.1 | async-start | bytes 1572864 | tf_op jit(solution)/shard_map/psum | solution.py:38
  8.1 9.5 %collective-permute-start = (s32[2,7]{1,0:T(2,128)S(1)}, s32[2,7]{1,0:T(2,128)S(1)}, u32[]{:S(2)}, u32[]{:S(2)}) collective-permute-start(s32[2,7]{1,0:T(2,128)S(1)} %get-tuple-element.250), channel_id=1, source_target_pairs={{0,1},{1,2},{2,3},{3,4},{4,5},{5,6},{6,7},{7,8},{8,9},{9,10},{10,1... | collective-permute-start | bytes 176 | tf_op jit(solution)/shard_map/ppermute | solution.py:16
  12.9 5.5 %collective-permute-start.1 = (s32[2,7]{1,0:T(2,128)S(1)}, s32[2,7]{1,0:T(2,128)S(1)}, u32[]{:S(2)}, u32[]{:S(2)}) collective-permute-start(s32[2,7]{1,0:T(2,128)S(1)} %get-tuple-element.251), channel_id=1, source_target_pairs={{1,0},{2,1},{3,2},{4,3},{5,4},{6,5},{7,6},{8,7},{9,8},{10,9},{11,1... | collective-permute-start | bytes 176 | tf_op jit(solution)/shard_map/ppermute | solution.py:17
  20.5 72.9 %copy-start = (bf16[512,1536]{1,0:T(8,128)(2,1)}, bf16[512,1536]{1,0:T(8,128)(2,1)S(1)}, u32[]{:S(2)}) copy-start(bf16[512,1536]{1,0:T(8,128)(2,1)S(1)} %get-tuple-element.255) | copy-start | bytes 4718596
  20.8 72.6 %copy-start.5 = (f32[1536]{0:T(1024)S(1)}, f32[1536]{0:T(1024)}, u32[]{:S(2)}) copy-start(f32[1536]{0:T(1024)} %get-tuple-element.200) | copy-start | bytes 18436
  20.8 72.6 %copy-start.6 = (f32[1536]{0:T(1024)S(1)}, f32[1536]{0:T(1024)}, u32[]{:S(2)}) copy-start(f32[1536]{0:T(1024)} %get-tuple-element.201) | copy-start | bytes 18436
  20.8 72.6 %copy-start.7 = (f32[1536]{0:T(1024)S(1)}, f32[1536]{0:T(1024)}, u32[]{:S(2)}) copy-start(f32[1536]{0:T(1024)} %get-tuple-element.202) | copy-start | bytes 18436
  20.8 8.9 %collective-permute-start.2 = (bf16[4,1536]{1,0:T(4,128)(2,1)S(1)}, bf16[4,1536]{1,0:T(4,128)(2,1)S(1)}, u32[]{:S(2)}, u32[]{:S(2)}) collective-permute-start(bf16[4,1536]{1,0:T(4,128)(2,1)S(1)} %get-tuple-element.248), channel_id=1, source_target_pairs={{0,1},{1,2},{2,3},{3,4},{4,5},{5,6},{6,7},{7,8},{8,9},{9,10},{10,1... | collective-permute-start | bytes 36872 | tf_op jit(solution)/shard_map/ppermute | solution.py:16
  25.3 5.6 %collective-permute-start.3 = (bf16[4,1536]{1,0:T(4,128)(2,1)S(1)}, bf16[4,1536]{1,0:T(4,128)(2,1)S(1)}, u32[]{:S(2)}, u32[]{:S(2)}) collective-permute-start(bf16[4,1536]{1,0:T(4,128)(2,1)S(1)} %get-tuple-element.249), channel_id=1, source_target_pairs={{1,0},{2,1},{3,2},{4,3},{5,4},{6,5},{7,6},{8,7},{9,8},{10,9},{11,1... | collective-permute-start | bytes 36872 | tf_op jit(solution)/shard_map/ppermute | solution.py:17
  29.7 63.6 %copy-start.10 = (bf16[4,1536]{1,0:T(4,128)(2,1)}, bf16[4,1536]{1,0:T(4,128)(2,1)S(1)}, u32[]{:S(2)}) copy-start(bf16[4,1536]{1,0:T(4,128)(2,1)S(1)} %collective-permute-done.2) | copy-start | bytes 36868
  30.9 62.5 %copy-start.11 = (bf16[4,1536]{1,0:T(4,128)(2,1)}, bf16[4,1536]{1,0:T(4,128)(2,1)S(1)}, u32[]{:S(2)}) copy-start(bf16[4,1536]{1,0:T(4,128)(2,1)S(1)} %collective-permute-done.3) | copy-start | bytes 36868
  109.1 6.1 %collective-permute-start.4 = (bf16[256,1536]{1,0:T(8,128)(2,1)}, bf16[256,1536]{1,0:T(8,128)(2,1)}, u32[]{:S(2)}, u32[]{:S(2)}) collective-permute-start(bf16[256,1536]{1,0:T(8,128)(2,1)} %reduce_max.45), channel_id=1, source_target_pairs={{0,16},{1,17},{2,18},{3,19},{4,20},{5,21},{6,22},{7,23},{8,24},{9,... | collective-permute-start | bytes 2359304 | tf_op jit(solution)/shard_map/ppermute | solution.py:33
  112.6 1.4 copy-start.1
  114.1 11.1 %copy-start.2 = (bf16[1,5,1536]{2,1,0:T(8,128)(2,1)S(1)}, bf16[1,5,1536]{2,1,0:T(8,128)(2,1)}, u32[]{:S(2)}) copy-start(bf16[1,5,1536]{2,1,0:T(8,128)(2,1)} %param.16) | copy-start | bytes 46084
  116.3 4.7 %collective-permute-start.5 = (bf16[4,1536]{1,0:T(4,128)(2,1)S(1)}, bf16[4,1536]{1,0:T(4,128)(2,1)S(1)}, u32[]{:S(2)}, u32[]{:S(2)}) collective-permute-start(bf16[4,1536]{1,0:T(4,128)(2,1)S(1)} %get-tuple-element.247), channel_id=1, source_target_pairs={{0,1},{1,2},{2,3},{3,4},{4,5},{5,6},{6,7},{7,8},{8,9},{9,10},{10,1... | collective-permute-start | bytes 36872 | tf_op jit(solution)/shard_map/while/body/eval_jaxpr/ppermute | solution.py:16
  119.6 5.6 %collective-permute-start.6 = (bf16[4,1536]{1,0:T(4,128)(2,1)S(1)}, bf16[4,1536]{1,0:T(4,128)(2,1)S(1)}, u32[]{:S(2)}, u32[]{:S(2)}) collective-permute-start(bf16[4,1536]{1,0:T(4,128)(2,1)S(1)} %get-tuple-element.246), channel_id=1, source_target_pairs={{1,0},{2,1},{3,2},{4,3},{5,4},{6,5},{7,6},{8,7},{9,8},{10,9},{11,1... | collective-permute-start | bytes 36872 | tf_op jit(solution)/shard_map/while/body/eval_jaxpr/ppermute | solution.py:17
  125.2 2.3 %copy-start.8 = (bf16[1536,1536]{1,0:T(8,128)(2,1)S(1)}, bf16[1536,1536]{1,0:T(8,128)(2,1)}, u32[]{:S(2)}) copy-start(bf16[1536,1536]{1,0:T(8,128)(2,1)} %get-tuple-element.139) | copy-start | bytes 14155780 | tf_op jit(solution)/shard_map/while/body/eval_jaxpr/cond/branch_1_fun/cond
  143.5 3.4 %collective-permute-start.7 = (bf16[256,1536]{1,0:T(8,128)(2,1)}, bf16[256,1536]{1,0:T(8,128)(2,1)S(1)}, u32[]{:S(2)}, u32[]{:S(2)}) collective-permute-start(bf16[256,1536]{1,0:T(8,128)(2,1)} %get-tuple-element.177), channel_id=1, source_target_pairs={{0,16},{1,17},{2,18},{3,19},{4,20},{5,21},{6,22},{7,23},{8,24},{9,... | collective-permute-start | bytes 2359304 | tf_op jit(solution)/shard_map/while/body/eval_jaxpr/ppermute | solution.py:33
  147.2 5.8 %collective-permute-start.8 = (bf16[4,1536]{1,0:T(4,128)(2,1)S(1)}, bf16[4,1536]{1,0:T(4,128)(2,1)S(1)}, u32[]{:S(2)}, u32[]{:S(2)}) collective-permute-start(bf16[4,1536]{1,0:T(4,128)(2,1)S(1)} %get-tuple-element.245), channel_id=1, source_target_pairs={{0,1},{1,2},{2,3},{3,4},{4,5},{5,6},{6,7},{7,8},{8,9},{9,10},{10,1... | collective-permute-start | bytes 36872 | tf_op jit(solution)/shard_map/ppermute | solution.py:16
  151.5 5.7 %collective-permute-start.9 = (bf16[4,1536]{1,0:T(4,128)(2,1)S(1)}, bf16[4,1536]{1,0:T(4,128)(2,1)}, u32[]{:S(2)}, u32[]{:S(2)}) collective-permute-start(bf16[4,1536]{1,0:T(4,128)(2,1)S(1)} %get-tuple-element.244), channel_id=1, source_target_pairs={{1,0},{2,1},{3,2},{4,3},{5,4},{6,5},{7,6},{8,7},{9,8},{10,9},{11,1... | collective-permute-start | bytes 36872 | tf_op jit(solution)/shard_map/ppermute | solution.py:17
Sparse Core Ops, SparseCore 0:
  10.2 83.1 all-gather.1
  160.5 30.5 all-reduce.3
where the time goes:
time: 203 us; the launch traced here: 200 us
  waiting for transfers between devices  106 us (52%)
  starting transfers between devices  26.4 us (13%)
  other arithmetic  22.1 us (11%)
  matrix products  16.9 us (8%)
  between operations  14.1 us (7%)
  local copies, waits for them, and re-layouts  12.6 us (6%)
    all_gather x1, waiting for transfers between devices, shards(): weights_full = lax.all_gather(point_weight, 'seq', axis=1, tiled=True)[0]  62.5 us
    psum x1, waiting for transfers between devices, from_root(): return lax.psum(kept, axis)  30.7 us
    ppermute x4, starting transfers between devices, padded(): before = lax.ppermute(last, axis, up)  16.9 us
    reduce_max x2, other arithmetic, halve_rows(): return jnp.max(rows.reshape(rows.shape[0] // 2, 2, rows.shape[1]), axis=1)  10.6 us
    ppermute x4, waiting for transfers between devices, padded(): after = lax.ppermute(first, axis, down)  10.4 us
    dot_general x1, matrix products, shards(): jnp.dot(filtered_first, weights_full, preferred_element_type=jnp.float32)  9.69 us
    dot_general x1, matrix products, run(): jnp.dot(filtered, weights_full, preferred_element_type=jnp.float32)  6.04 us
    ppermute x4, starting transfers between devices, padded(): after = lax.ppermute(first, axis, down)  5.75 us
  transfers between devices with their start and end apart: 12, of which 8 were waited for; matrix products, arithmetic and copies ran while one was open for 6% of the time, Pallas kernels for 0%

commit v1 on v0

--- a/solution.py
+++ b/solution.py
@@ -1,6 +1,10 @@
+import functools
+
 import jax
 import jax.numpy as jnp
 from jax import lax
+from jax.experimental import pallas as pl
+from jax.experimental.pallas import tpu as pltpu
 from jax.sharding import PartitionSpec as P
 
 DILATION_STEP = 2
@@ -175,9 +179,390 @@
     return lax.dynamic_slice_in_dim(coarsest, position * out_width, out_width, 2)
 
 
+GROUP = 4
+BLOCK = 16
+MESH = pl.DeviceIdType.MESH
+
+
+def gelu_of(scaled):
+    inner = scaled * (0.7978845608028654 + 0.03567740813636141 * (scaled * scaled))
+    return (0.5 * scaled) * (1.0 + jnp.tanh(inner))
+
+
+def encoder_kernel(
+    n_seq,
+    runs,
+    taps,
+    ids_ref,
+    stem_ref,
+    params_ref,
+    weight_ref,
+    out_ref,
+    ids_all,
+    params_all,
+    one_hot,
+    window,
+    x0_buf,
+    act_buf,
+    d0_buf,
+    x1_buf,
+    d1_buf,
+    weights,
+    send_sem,
+    recv_sem,
+    side_send,
+    side_recv,
+    local_sem,
+    half_send,
+    half_recv,
+):
+    j = lax.axis_index("section")
+    q = lax.axis_index("seq")
+    n_z = n_seq // 4
+    x, y, z = lax.rem(q, 2), lax.rem(lax.div(q, 2), 2), lax.div(q, 4)
+    to_x, to_y = 1 - 2 * x, 2 * (1 - 2 * y)
+    to_a = (1 - j) * to_x + j * to_y
+    to_b = j * to_x + (1 - j) * to_y
+    right, left = lax.rem(q + 1, n_seq), lax.rem(q + n_seq - 1, n_seq)
+    other = 1 - j
+    depth, width = weight_ref.shape[1], weight_ref.shape[2] // 2
+    channels = 2 * width
+    rows = x0_buf.shape[1]
+    margin = (rows - runs) // 2
+    sequences = out_ref.shape[0]
+
+    def at_z(offset):
+        return lax.rem(z + offset, n_z) * 4 + lax.rem(q, 4)
+
+    barrier = pltpu.get_barrier_semaphore()
+    greeted = [(other, q), (j, q + to_a), (j, q + to_b), (j, left), (j, right)]
+    greeted += [(j, at_z(offset)) for offset in range(1, n_z)]
+    for device in greeted:
+        pl.semaphore_signal(barrier, inc=1, device_id=device, device_id_type=MESH)
+    pl.semaphore_wait(barrier, len(greeted))
+
+    def remote(src, dst, send, recv, device):
+        return pltpu.make_async_remote_copy(
+            src_ref=src,
+            dst_ref=dst,
+            send_sem=send,
+            recv_sem=recv,
+            device_id=device,
+            device_id_type=MESH,
+        )
+
+    def chunk(level, index):
+        start = pl.multiple_of(index * depth, BLOCK)
+        return weights.at[level, pl.ds(start, depth)]
+
+    def columns(half):
+        return pl.ds(pl.multiple_of(half * width, 128), width)
+
+    local = pltpu.make_async_copy(
+        weight_ref.at[0, :, columns(j)], chunk(j, q), local_sem.at[0]
+    )
+    swap = remote(
+        weight_ref.at[0, :, columns(other)], chunk(j, q), side_send.at[0], side_recv.at[0], (other, q)
+    )
+    swapped = remote(
+        weight_ref.at[0, :, columns(other)],
+        chunk(other, q),
+        side_send.at[0],
+        side_recv.at[0],
+        (other, q),
+    )
+    swap.start()
+    local.start()
+    to_right = remote(ids_ref, ids_all.at[0], side_send.at[1], side_recv.at[1], (j, right))
+    to_left = remote(ids_ref, ids_all.at[2], side_send.at[2], side_recv.at[2], (j, left))
+    to_right.start()
+    to_left.start()
+    share = remote(params_ref, params_all.at[j], side_send.at[3], side_recv.at[3], (other, q))
+    shared = remote(params_ref, params_all.at[other], side_send.at[3], side_recv.at[3], (other, q))
+    share.start()
+    keep = pltpu.make_async_copy(params_ref, params_all.at[j], local_sem.at[1])
+    keep.start()
+    keep_ids = pltpu.make_async_copy(ids_ref, ids_all.at[1], local_sem.at[2])
+    keep_ids.start()
+
+    def z_copy(level, offset, incoming):
+        index = at_z(n_z - offset) if incoming else q
+        slot = offset - 1
+        part = chunk(level, index)
+        return remote(
+            part, part, send_sem.at[level, slot], recv_sem.at[level, slot], (j, at_z(offset))
+        )
+
+    def a_copy(level, offset, incoming):
+        index = at_z(n_z - offset) if offset else q
+        slot = n_z - 1 + offset
+        part = chunk(level, index + to_a if incoming else index)
+        return remote(
+            part, part, send_sem.at[level, slot], recv_sem.at[level, slot], (j, q + to_a)
+        )
+
+    def b_copy(level, offset, crossed, incoming):
+        index = at_z(n_z - offset) if offset else q
+        index = index + to_a if crossed else index
+        slot = 2 * n_z - 1 + offset + (n_z if crossed else 0)
+        part = chunk(level, index + to_b if incoming else index)
+        return remote(
+            part, part, send_sem.at[level, slot], recv_sem.at[level, slot], (j, q + to_b)
+        )
+
+    def own(level):
+        for offset in range(1, n_z):
+            z_copy(level, offset, False).start()
+        a_copy(level, 0, False).start()
+        b_copy(level, 0, False, False).start()
+
+    def z_event(level, offset):
+        z_copy(level, offset, True).wait_recv()
+        a_copy(level, offset, False).start()
+        b_copy(level, offset, False, False).start()
+
+    def a_event(level, offset):
+        a_copy(level, offset, True).wait_recv()
+        b_copy(level, offset, True, False).start()
+
+    def b_events(level):
+        for offset in range(n_z):
+            b_copy(level, offset, False, True).wait_recv()
+        for offset in range(n_z):
+            b_copy(level, offset, True, True).wait_recv()
+
+    def sends_done(level):
+        for offset in range(1, n_z):
+            z_copy(level, offset, False).wait_send()
+        for offset in range(n_z):
+            a_copy(level, offset, False).wait_send()
+            b_copy(level, offset, False, False).wait_send()
+            b_copy(level, offset, True, False).wait_send()
+
+    to_right.wait_recv()
+    to_left.wait_recv()
+    keep_ids.wait()
+    here = jnp.concatenate(
+        [
+            jnp.where(q > 0, ids_all[0], -1),
+            ids_all[1],
+            jnp.where(q < n_seq - 1, ids_all[2], -1),
+        ],
+        axis=1,
+    )
+    lanes = here.shape[1]
+    span = one_hot.shape[1]
+    four = lax.broadcasted_iota(jnp.int32, (4, span), 0)
+    one_hot[...] = jnp.zeros_like(one_hot)
+    rolled = {}
+    for b in range(sequences):
+        for c in range(GROUP):
+            for k in range(taps):
+                away = c + k - taps // 2
+                shift, klass = away // GROUP, b * GROUP + away % GROUP
+                if shift not in rolled:
+                    begin = runs - margin + shift
+                    rolled[shift] = pltpu.roll(here, (lanes - begin) % lanes, 1)
+                line = rolled[shift][klass : klass + 1, :span]
+                hit = jnp.broadcast_to(line, (4, span)) == four
+                one_hot[4 * k : 4 * k + 4, :] = hit.astype(jnp.float32)
+            window[b * GROUP + c] = one_hot[...].T[:rows].astype(jnp.bfloat16)
+
+    local.wait()
+    swapped.wait_recv()
+    own(0)
+    own(1)
+    keep.wait()
+    shared.wait_recv()
+
+    def row_mask(start, total_low, total_high, count):
+        index = lax.broadcasted_iota(jnp.int32, (count, 1), 0) + start
+        return (index >= total_low) & (index < total_high)
+
+    low = margin - q * runs
+    high = low + n_seq * runs
+    blocks = rows // BLOCK
+    inverse = 1.0 / channels
+
+    def first_block(step, carry):
+        stream = lax.div(step, blocks)
+        start = pl.multiple_of(lax.rem(step, blocks) * BLOCK, BLOCK)
+        part = pl.ds(start, BLOCK)
+        found = jnp.dot(
+            window[stream, part, :], stem_ref[...], preferred_element_type=jnp.float32
+        ).astype(jnp.bfloat16)
+        x0_buf[stream, part, :] = found
+        values = found.astype(jnp.float32)
+        mean = jnp.sum(values * values, axis=1, keepdims=True) * inverse
+        scaled = values * lax.rsqrt(mean + 1e-06) * params_all[0, 0:1, :]
+        act_buf[stream, part, :] = jnp.where(
+            row_mask(start, low, high, BLOCK), gelu_of(scaled), 0.0
+        )
+        return carry
+
+    col_blocks = channels // 128
+
+    def first_filter(step, carry):
+        col = pl.ds(pl.multiple_of(lax.rem(step, col_blocks) * 128, 128), 128)
+        pair = lax.div(step, col_blocks)
+        even = lax.div(pair, 2) * GROUP + lax.rem(pair, 2)
+        odd = even + 2
+        tap = [params_all[0, 1 + k : 2 + k, col] for k in range(5)]
+        a0, a2 = act_buf[even, :, col], act_buf[odd, :, col]
+        a0_before, a2_before = pltpu.roll(a0, 1, 0), pltpu.roll(a2, 1, 0)
+        a0_after, a2_after = pltpu.roll(a0, rows - 1, 0), pltpu.roll(a2, rows - 1, 0)
+        d0_buf[even, :, col] = (
+            tap[0] * a0_before + tap[1] * a2_before + tap[2] * a0 + tap[3] * a2 + tap[4] * a0_after
+        ).astype(jnp.bfloat16)
+        d0_buf[odd, :, col] = (
+            tap[0] * a2_before + tap[1] * a0 + tap[2] * a2 + tap[3] * a0_after + tap[4] * a2_after
+        ).astype(jnp.bfloat16)
+        return carry
+
+    def interleaved(total, body, events):
+        done = 0
+        for number, event in enumerate(events):
+            until = total * (number + 1) // (len(events) + 1)
+            lax.fori_loop(done, until, body, 0)
+            event()
+            done = until
+        lax.fori_loop(done, total, body, 0)
+
+    def later(function, *args):
+        return lambda: function(*args)
+
+    z_events = [[later(z_event, level, o) for o in range(1, n_z)] for level in range(2)]
+    a_events = [[later(a_event, level, o) for o in range(n_z)] for level in range(2)]
+
+    interleaved(sequences * GROUP * blocks, first_block, z_events[0] + a_events[0])
+    interleaved(sequences * 2 * col_blocks, first_filter, z_events[1] + a_events[1])
+
+    def half_copy(stream, incoming):
+        part = x1_buf.at[stream, other if incoming else j]
+        return remote(part, part, half_send.at[stream], half_recv.at[stream], (other, q))
+
+    b_events(0)
+    for stream in range(2 * sequences):
+        taken = d0_buf[2 * stream : 2 * stream + 2].reshape(2 * rows, channels)
+        product = jnp.dot(taken, weights[0], preferred_element_type=jnp.float32)
+        level_rows = x0_buf[2 * stream : 2 * stream + 2, :, columns(j)].reshape(2 * rows, width)
+        mixed = (level_rows.astype(jnp.float32) + product).astype(jnp.bfloat16)
+        x1_buf[stream, j] = jnp.maximum(mixed[:rows], mixed[rows:])
+        half_copy(stream, False).start()
+
+    def second_block(stream):
+        def run(step, carry):
+            start = pl.multiple_of(step * BLOCK, BLOCK)
+            part = pl.ds(start, BLOCK)
+            values = jnp.concatenate(
+                [x1_buf[stream, 0, part, :], x1_buf[stream, 1, part, :]], axis=1
+            ).astype(jnp.float32)
+            mean = jnp.sum(values * values, axis=1, keepdims=True) * inverse
+            scaled = values * lax.rsqrt(mean + 1e-06) * params_all[1, 0:1, :]
+            act_buf[stream, part, :] = jnp.where(
+                row_mask(start, low, high, BLOCK), gelu_of(scaled), 0.0
+            )
+            return carry
+
+        return run
+
+    def second_filter(stream):
+        def run(step, carry):
+            col = pl.ds(pl.multiple_of(step * 128, 128), 128)
+            tap = [params_all[1, 1 + k : 2 + k, col] for k in range(5)]
+            a = act_buf[stream, :, col]
+            total = tap[2] * a
+            for k in (0, 1, 3, 4):
+                total = total + tap[k] * pltpu.roll(a, (2 - k) % rows, 0)
+            d1_buf[stream, :, col] = total[margin : margin + runs].astype(jnp.bfloat16)
+            return carry
+
+        return run
+
+    for stream in range(2 * sequences):
+        half_copy(stream, True).wait_recv()
+        lax.fori_loop(0, blocks, second_block(stream), 0)
+        lax.fori_loop(0, col_blocks, second_filter(stream), 0)
+
+    b_events(1)
+    for b in range(sequences):
+        taken = d1_buf[2 * b : 2 * b + 2].reshape(2 * runs, channels)
+        product = jnp.dot(taken, weights[1], preferred_element_type=jnp.float32)
+        level_rows = x1_buf[2 * b : 2 * b + 2, j, margin : margin + runs, :]
+        level_rows = level_rows.reshape(2 * runs, width)
+        mixed = (level_rows.astype(jnp.float32) + product).astype(jnp.bfloat16)
+        out_ref[b] = jnp.maximum(mixed[:runs], mixed[runs:])
+
+    swap.wait_send()
+    to_right.wait_send()
+    to_left.wait_send()
+    share.wait_send()
+    for stream in range(2 * sequences):
+        half_copy(stream, False).wait_send()
+    sends_done(0)
+    sends_done(1)
+
+
+def fused(bases, stem_weight, gains, depth_taps, point_weight):
+    n_seq = lax.axis_size("seq")
+    sequences, width_rows = bases.shape
+    taps, kinds, channels = stem_weight.shape
+    runs = width_rows // GROUP
+    rows = runs + BLOCK
+    streams = sequences * GROUP
+    ids = bases.reshape(sequences, runs, GROUP).transpose(0, 2, 1).reshape(streams, runs)
+    stem = jnp.pad(stem_weight.reshape(taps * kinds, channels), ((0, 128 - taps * kinds), (0, 0)))
+    params = jnp.concatenate([gains, depth_taps[0]], axis=0).astype(jnp.float32)
+    params = jnp.pad(params, ((0, 8 - params.shape[0]), (0, 0)))
+    half = channels // 2
+    n_z = n_seq // 4
+    slots = 4 * n_z - 1
+    vmem = pl.BlockSpec(memory_space=pltpu.VMEM)
+    dma = pltpu.SemaphoreType.DMA
+    return pl.pallas_call(
+        functools.partial(encoder_kernel, n_seq, runs, taps),
+        out_shape=jax.ShapeDtypeStruct((sequences, runs, half), jnp.bfloat16),
+        in_specs=[vmem] * 4,
+        out_specs=vmem,
+        scratch_shapes=[
+            pltpu.VMEM((3, streams, runs), jnp.int32),
+            pltpu.VMEM((2, 8, channels), jnp.float32),
+            pltpu.VMEM((128, 2 * runs), jnp.float32),
+            pltpu.VMEM((streams, rows, 128), jnp.bfloat16),
+            pltpu.VMEM((streams, rows, channels), jnp.bfloat16),
+            pltpu.VMEM((streams, rows, channels), jnp.float32),
+            pltpu.VMEM((streams, rows, channels), jnp.bfloat16),
+            pltpu.VMEM((streams // 2, 2, rows, half), jnp.bfloat16),
+            pltpu.VMEM((streams // 2, runs, channels), jnp.bfloat16),
+            pltpu.VMEM((2, channels, half), jnp.bfloat16),
+            dma((2, slots)),
+            dma((2, slots)),
+            dma((4,)),
+            dma((4,)),
+            dma((3,)),
+            dma((streams // 2,)),
+            dma((streams // 2,)),
+        ],
+        compiler_params=pltpu.CompilerParams(
+            collective_id=0, has_side_effects=True, vmem_limit_bytes=56 * 1024 * 1024
+        ),
+    )(ids, stem, params, point_weight)
+
+
+def chosen(bases, stem_weight, gains, depth_taps, point_weight):
+    n_seq = lax.axis_size("seq")
+    taps, kinds, channels = stem_weight.shape
+    fits = lax.axis_size("section") == 2 and n_seq % 4 == 0 and depth_taps.shape[1] == 5
+    fits = fits and bases.shape[1] == GROUP * 128 and (bases.shape[0] * GROUP) % 8 == 0
+    fits = fits and channels % 256 == 0 and point_weight.shape[1] % BLOCK == 0
+    fits = fits and kinds == 4 and taps * kinds <= 128
+    run = fused if fits else shards
+    return run(bases, stem_weight, gains, depth_taps, point_weight)
+
+
 def solution(mesh):
     return jax.shard_map(
-        shards,
+        chosen,
         mesh=mesh,
         in_specs=(
             P(None, "seq"),

time: 203 us -> 74.9 us (0.37)
  the two profiles are of different devices: /device:TPU:0 before, /device:TPU:12 now
where the time goes in v1:
time: 74.9 us; the launch traced here: 74.7 us
  Pallas kernels  69.1 us (92%)
  local copies, waits for them, and re-layouts  4.08 us (5%)
  other arithmetic  1.42 us (2%)
    pallas_call x1, Pallas kernels, fused(): pl.pallas_call(functools.partial(encoder_kernel, n_seq, runs, taps), out_...  69.1 us
    unnamed x3, local copies, waits for them, and re-layouts  1.77 us

profile of v1, /device:TPU:12, one launch (start us, length us, event | category | flops | bytes accessed | tf_op | source)
XLA Modules:
  0.0 74.7 jit_solution(9067449655395323500)
XLA Ops:
  0.0 0.0 copy-start
  0.0 1.4 %fusion.3.params_ref = f32[8,1536]{1,0:T(8,128)} fusion(bf16[5,1536]{1,0:T(8,128)(2,1)} %bitcast.4, bf16[1,1536]{1,0:T(2,128)(2,1)} %param.7), kind=kLoop, calls=%fused_computation.4 | loop fusion | flops 86016 | bytes 67584 | tf_op jit(solution)/shard_map/jit(_pad)/pad | solution.py:516
  1.4 0.8 %reshape.9 = s32[2,128,4]{2,1,0:T(8,128)S(1)} reshape(s32[2,512]{1,0:T(2,128)} %param.5) | data formatting | bytes 8192 | tf_op jit(solution)/shard_map/reshape | solution.py:513
  2.3 0.7 copy.7
  2.9 0.0 copy-done
  3.0 0.8 %pad.10.stem_ref = bf16[128,1536]{1,0:T(8,128)(2,1)} pad(bf16[60,1536]{1,0:T(8,128)(2,1)S(1)} %reshape.11, bf16[]{:T(256)} %constant.4.clone.1), padding=0_68x0_0 | pad | bytes 577538 | tf_op jit(solution)/shard_map/jit(_pad)/pad | solution.py:514
  3.7 69.1 %shard_map.55 = bf16[2,128,768]{2,1,0:T(8,128)(2,1)} custom-call(s32[8,128]{1,0:T(8,128)} %bitcast.5, bf16[128,1536]{1,0:T(8,128)(2,1)} %pad.10.stem_ref, f32[8,1536]{1,0:T(8,128)} %fusion.3.params_ref, bf16[1,96,1536]{2,1,0:T(8,128)(2,1)} %weight_ref.1), custom_call_target="tpu_custom_call" | custom-call | tf_op jit(solution)/shard_map/pallas_call | solution.py:522
  72.9 1.8 %copy.9 = bf16[2,128,768]{2,1,0:T(8,128)(2,1)} copy(bf16[2,128,768]{2,1,0:T(8,128)(2,1)} %shard_map.55) | data formatting | bytes 786432
  (1 shorter events, 0.0 us)
Async XLA Ops:
  0.0 2.9 %copy-start = (bf16[15,4,1536]{2,1,0:T(4,128)(2,1)S(1)}, bf16[15,4,1536]{2,1,0:T(4,128)(2,1)}, u32[]{:S(2)}) copy-start(bf16[15,4,1536]{2,1,0:T(4,128)(2,1)} %param.6) | copy-start | bytes 552964

commit v2 on v1

--- a/solution.py
+++ b/solution.py
@@ -181,6 +181,7 @@
 
 GROUP = 4
 BLOCK = 16
+PART = 48
 MESH = pl.DeviceIdType.MESH
 
 
@@ -191,16 +192,18 @@
 
 def encoder_kernel(
     n_seq,
-    runs,
-    taps,
-    ids_ref,
+    bases_ref,
     stem_ref,
-    params_ref,
+    gains_ref,
+    taps_ref,
     weight_ref,
     out_ref,
     ids_all,
     params_all,
+    stem_wide,
+    stem_flat,
     one_hot,
+    one_hot_rows,
     window,
     x0_buf,
     act_buf,
@@ -208,13 +211,16 @@
     x1_buf,
     d1_buf,
     weights,
+    stage,
     send_sem,
     recv_sem,
+    pair_send,
+    pair_recv,
     side_send,
     side_recv,
     local_sem,
-    half_send,
-    half_recv,
+    out_send,
+    out_recv,
 ):
     j = lax.axis_index("section")
     q = lax.axis_index("seq")
@@ -227,10 +233,12 @@
     other = 1 - j
     depth, width = weight_ref.shape[1], weight_ref.shape[2] // 2
     channels = 2 * width
+    taps = stem_ref.shape[0]
     rows = x0_buf.shape[1]
+    sequences, length = bases_ref.shape
+    runs = length // GROUP
     margin = (rows - runs) // 2
-    sequences = out_ref.shape[0]
-
+    mine = sequences // 2
     def at_z(offset):
         return lax.rem(z + offset, n_z) * 4 + lax.rem(q, 4)
 
@@ -251,44 +259,71 @@
             device_id_type=MESH,
         )
 
-    def chunk(level, index):
+    def chunk(level, index, half):
         start = pl.multiple_of(index * depth, BLOCK)
-        return weights.at[level, pl.ds(start, depth)]
-
-    def columns(half):
-        return pl.ds(pl.multiple_of(half * width, 128), width)
-
-    local = pltpu.make_async_copy(
-        weight_ref.at[0, :, columns(j)], chunk(j, q), local_sem.at[0]
-    )
-    swap = remote(
-        weight_ref.at[0, :, columns(other)], chunk(j, q), side_send.at[0], side_recv.at[0], (other, q)
-    )
-    swapped = remote(
-        weight_ref.at[0, :, columns(other)],
-        chunk(other, q),
-        side_send.at[0],
-        side_recv.at[0],
-        (other, q),
-    )
-    swap.start()
-    local.start()
-    to_right = remote(ids_ref, ids_all.at[0], side_send.at[1], side_recv.at[1], (j, right))
-    to_left = remote(ids_ref, ids_all.at[2], side_send.at[2], side_recv.at[2], (j, left))
+        return weights.at[level, half, pl.ds(start, depth)]
+
+    def block(half):
+        return weight_ref.at[0, :, half * width : (half + 1) * width]
+
+    def other_block():
+        return weight_ref.at[0, :, pl.ds(pl.multiple_of(other * width, 128), width)]
+
+    def own_block():
+        return weight_ref.at[0, :, pl.ds(pl.multiple_of(j * width, 128), width)]
+
+    swap = [
+        remote(src, chunk(j, q, h), side_send.at[n], side_recv.at[n], (other, q))
+        for n, (src, h) in enumerate([(other_block(), other), (own_block(), j)])
+    ]
+    swapped = [
+        remote(src, chunk(other, q, h), side_send.at[n], side_recv.at[n], (other, q))
+        for n, (src, h) in enumerate([(own_block(), j), (other_block(), other)])
+    ]
+    local = [
+        pltpu.make_async_copy(block(h), chunk(j, q, h), local_sem.at[h]) for h in range(2)
+    ]
+    edge = 128
+    to_right = remote(
+        bases_ref.at[:, length - edge :],
+        ids_all.at[:, :edge],
+        side_send.at[2],
+        side_recv.at[2],
+        (j, right),
+    )
+    to_left = remote(
+        bases_ref.at[:, :edge],
+        ids_all.at[:, edge + length :],
+        side_send.at[3],
+        side_recv.at[3],
+        (j, left),
+    )
+    swap[0].start()
     to_right.start()
     to_left.start()
-    share = remote(params_ref, params_all.at[j], side_send.at[3], side_recv.at[3], (other, q))
-    shared = remote(params_ref, params_all.at[other], side_send.at[3], side_recv.at[3], (other, q))
+    for h in range(2):
+        local[h].start()
+    keep_ids = pltpu.make_async_copy(
+        bases_ref, ids_all.at[:, edge : edge + length], local_sem.at[2]
+    )
+    keep_ids.start()
+    params_all[j, 0:1, :] = gains_ref[...].astype(jnp.float32)
+    params_all[j, 1:6, :] = taps_ref[0].astype(jnp.float32)
+    share = remote(
+        params_all.at[j], params_all.at[j], side_send.at[4], side_recv.at[4], (other, q)
+    )
+    shared = remote(
+        params_all.at[other], params_all.at[other], side_send.at[4], side_recv.at[4], (other, q)
+    )
     share.start()
-    keep = pltpu.make_async_copy(params_ref, params_all.at[j], local_sem.at[1])
-    keep.start()
-    keep_ids = pltpu.make_async_copy(ids_ref, ids_all.at[1], local_sem.at[2])
-    keep_ids.start()
+    for h in range(2):
+        local[h].wait()
+    swapped[0].wait_recv()
 
     def z_copy(level, offset, incoming):
         index = at_z(n_z - offset) if incoming else q
         slot = offset - 1
-        part = chunk(level, index)
+        part = chunk(level, index, j)
         return remote(
             part, part, send_sem.at[level, slot], recv_sem.at[level, slot], (j, at_z(offset))
         )
@@ -296,7 +331,7 @@
     def a_copy(level, offset, incoming):
         index = at_z(n_z - offset) if offset else q
         slot = n_z - 1 + offset
-        part = chunk(level, index + to_a if incoming else index)
+        part = chunk(level, index + to_a if incoming else index, j)
         return remote(
             part, part, send_sem.at[level, slot], recv_sem.at[level, slot], (j, q + to_a)
         )
@@ -305,10 +340,32 @@
         index = at_z(n_z - offset) if offset else q
         index = index + to_a if crossed else index
         slot = 2 * n_z - 1 + offset + (n_z if crossed else 0)
-        part = chunk(level, index + to_b if incoming else index)
+        part = chunk(level, index + to_b if incoming else index, j)
         return remote(
             part, part, send_sem.at[level, slot], recv_sem.at[level, slot], (j, q + to_b)
         )
+
+    def pair_copy(level, index, slot, incoming):
+        part = chunk(level, index, other if incoming else j)
+        return remote(
+            part, part, pair_send.at[level, slot], pair_recv.at[level, slot], (other, q)
+        )
+
+    def pair_index(slot, incoming):
+        step_a, step_b = (to_b, to_a) if incoming else (to_a, to_b)
+        if slot < n_z - 1:
+            return at_z(n_z - slot - 1)
+        offset = (slot - n_z + 1) % n_z
+        index = at_z(n_z - offset) if offset else q
+        kind = (slot - n_z + 1) // n_z
+        return index + (step_a, step_b, step_a + step_b)[kind]
+
+    def pair(level, slot, incoming=False):
+        return pair_copy(level, pair_index(slot, incoming), slot, incoming)
+
+    def pairs_in(level):
+        for slot in range(4 * n_z - 1):
+            pair(level, slot, True).wait_recv()
 
     def own(level):
         for offset in range(1, n_z):
@@ -320,16 +377,16 @@
         z_copy(level, offset, True).wait_recv()
         a_copy(level, offset, False).start()
         b_copy(level, offset, False, False).start()
+        pair(level, offset - 1).start()
 
     def a_event(level, offset):
         a_copy(level, offset, True).wait_recv()
         b_copy(level, offset, True, False).start()
-
-    def b_events(level):
-        for offset in range(n_z):
-            b_copy(level, offset, False, True).wait_recv()
-        for offset in range(n_z):
-            b_copy(level, offset, True, True).wait_recv()
+        pair(level, n_z - 1 + offset).start()
+
+    def b_event(level, offset, crossed):
+        b_copy(level, offset, crossed, True).wait_recv()
+        pair(level, (3 * n_z - 1 if crossed else 2 * n_z - 1) + offset).start()
 
     def sends_done(level):
         for offset in range(1, n_z):
@@ -338,41 +395,39 @@
             a_copy(level, offset, False).wait_send()
             b_copy(level, offset, False, False).wait_send()
             b_copy(level, offset, True, False).wait_send()
-
+        for slot in range(4 * n_z - 1):
+            pair(level, slot).wait_send()
+
+    own(0)
+    own(1)
+    swap[1].start()
+
+    stem_wide[...] = jnp.zeros_like(stem_wide)
+    one_hot[...] = jnp.zeros_like(one_hot)
+    for k in range(taps):
+        stem_wide[4 * k : 4 * k + 4, :] = stem_ref[k].astype(jnp.float32)
+    stem_flat[...] = stem_wide[...].astype(jnp.bfloat16)
     to_right.wait_recv()
     to_left.wait_recv()
     keep_ids.wait()
-    here = jnp.concatenate(
-        [
-            jnp.where(q > 0, ids_all[0], -1),
-            ids_all[1],
-            jnp.where(q < n_seq - 1, ids_all[2], -1),
-        ],
-        axis=1,
-    )
-    lanes = here.shape[1]
+    lanes = ids_all.shape[1]
     span = one_hot.shape[1]
     four = lax.broadcasted_iota(jnp.int32, (4, span), 0)
-    one_hot[...] = jnp.zeros_like(one_hot)
-    rolled = {}
-    for b in range(sequences):
+    place = lax.broadcasted_iota(jnp.int32, (1, lanes), 1)
+    inside = ((place >= edge) | (q > 0)) & ((place < edge + length) | (q < n_seq - 1))
+    for b in range(mine):
+        line = jnp.where(j == 0, ids_all[b : b + 1, :], ids_all[mine + b : mine + b + 1, :])
+        line = jnp.where(inside, line, -1)
+        for k in range(taps):
+            begin = edge - GROUP * margin + k - taps // 2
+            moved = pltpu.roll(line, lanes - begin, 1)[:, :span]
+            hit = jnp.broadcast_to(moved, (4, span)) == four
+            one_hot[4 * k : 4 * k + 4, :] = hit.astype(jnp.float32)
+        one_hot_rows[...] = one_hot[...].T
         for c in range(GROUP):
-            for k in range(taps):
-                away = c + k - taps // 2
-                shift, klass = away // GROUP, b * GROUP + away % GROUP
-                if shift not in rolled:
-                    begin = runs - margin + shift
-                    rolled[shift] = pltpu.roll(here, (lanes - begin) % lanes, 1)
-                line = rolled[shift][klass : klass + 1, :span]
-                hit = jnp.broadcast_to(line, (4, span)) == four
-                one_hot[4 * k : 4 * k + 4, :] = hit.astype(jnp.float32)
-            window[b * GROUP + c] = one_hot[...].T[:rows].astype(jnp.bfloat16)
-
-    local.wait()
-    swapped.wait_recv()
-    own(0)
-    own(1)
-    keep.wait()
+            window[b * GROUP + c] = one_hot_rows[pl.ds(c, rows, stride=GROUP), :].astype(
+                jnp.bfloat16
+            )
     shared.wait_recv()
 
     def row_mask(start, total_low, total_high, count):
@@ -381,22 +436,22 @@
 
     low = margin - q * runs
     high = low + n_seq * runs
-    blocks = rows // BLOCK
+    blocks = rows // PART
     inverse = 1.0 / channels
 
     def first_block(step, carry):
         stream = lax.div(step, blocks)
-        start = pl.multiple_of(lax.rem(step, blocks) * BLOCK, BLOCK)
-        part = pl.ds(start, BLOCK)
+        start = pl.multiple_of(lax.rem(step, blocks) * PART, PART)
+        part = pl.ds(start, PART)
         found = jnp.dot(
-            window[stream, part, :], stem_ref[...], preferred_element_type=jnp.float32
+            window[stream, part, :], stem_flat[...], preferred_element_type=jnp.float32
         ).astype(jnp.bfloat16)
         x0_buf[stream, part, :] = found
         values = found.astype(jnp.float32)
         mean = jnp.sum(values * values, axis=1, keepdims=True) * inverse
         scaled = values * lax.rsqrt(mean + 1e-06) * params_all[0, 0:1, :]
         act_buf[stream, part, :] = jnp.where(
-            row_mask(start, low, high, BLOCK), gelu_of(scaled), 0.0
+            row_mask(start, low, high, PART), gelu_of(scaled), 0.0
         )
         return carry
 
@@ -434,33 +489,38 @@
     z_events = [[later(z_event, level, o) for o in range(1, n_z)] for level in range(2)]
     a_events = [[later(a_event, level, o) for o in range(n_z)] for level in range(2)]
 
-    interleaved(sequences * GROUP * blocks, first_block, z_events[0] + a_events[0])
-    interleaved(sequences * 2 * col_blocks, first_filter, z_events[1] + a_events[1])
-
-    def half_copy(stream, incoming):
-        part = x1_buf.at[stream, other if incoming else j]
-        return remote(part, part, half_send.at[stream], half_recv.at[stream], (other, q))
-
-    b_events(0)
-    for stream in range(2 * sequences):
-        taken = d0_buf[2 * stream : 2 * stream + 2].reshape(2 * rows, channels)
-        product = jnp.dot(taken, weights[0], preferred_element_type=jnp.float32)
-        level_rows = x0_buf[2 * stream : 2 * stream + 2, :, columns(j)].reshape(2 * rows, width)
-        mixed = (level_rows.astype(jnp.float32) + product).astype(jnp.bfloat16)
-        x1_buf[stream, j] = jnp.maximum(mixed[:rows], mixed[rows:])
-        half_copy(stream, False).start()
+    b_early = [[later(b_event, level, o, False) for o in range(n_z)] for level in range(2)]
+    b_late = [[later(b_event, level, o, True) for o in range(n_z)] for level in range(2)]
+    interleaved(mine * GROUP * blocks, first_block, z_events[0] + a_events[0])
+    interleaved(
+        mine * 2 * col_blocks, first_filter, z_events[1] + b_early[0] + a_events[1] + b_late[0]
+    )
+
+    swapped[1].wait_recv()
+    pairs_in(0)
+    rest = b_early[1] + b_late[1]
+    for stream in range(2 * mine):
+        for h in range(2):
+            taken = d0_buf[2 * stream : 2 * stream + 2].reshape(2 * rows, channels)
+            product = jnp.dot(taken, weights[0, h], preferred_element_type=jnp.float32)
+            level_rows = x0_buf[2 * stream : 2 * stream + 2, :, h * width : (h + 1) * width]
+            level_rows = level_rows.reshape(2 * rows, width)
+            mixed = (level_rows.astype(jnp.float32) + product).astype(jnp.bfloat16)
+            x1_buf[stream, :, h * width : (h + 1) * width] = jnp.maximum(
+                mixed[:rows], mixed[rows:]
+            )
+            if rest:
+                rest.pop(0)()
 
     def second_block(stream):
         def run(step, carry):
-            start = pl.multiple_of(step * BLOCK, BLOCK)
-            part = pl.ds(start, BLOCK)
-            values = jnp.concatenate(
-                [x1_buf[stream, 0, part, :], x1_buf[stream, 1, part, :]], axis=1
-            ).astype(jnp.float32)
+            start = pl.multiple_of(step * PART, PART)
+            part = pl.ds(start, PART)
+            values = x1_buf[stream, part, :].astype(jnp.float32)
             mean = jnp.sum(values * values, axis=1, keepdims=True) * inverse
             scaled = values * lax.rsqrt(mean + 1e-06) * params_all[1, 0:1, :]
             act_buf[stream, part, :] = jnp.where(
-                row_mask(start, low, high, BLOCK), gelu_of(scaled), 0.0
+                row_mask(start, low, high, PART), gelu_of(scaled), 0.0
             )
             return carry
 
@@ -479,26 +539,44 @@
 
         return run
 
-    for stream in range(2 * sequences):
-        half_copy(stream, True).wait_recv()
+    for stream in range(2 * mine):
         lax.fori_loop(0, blocks, second_block(stream), 0)
+        if rest:
+            rest.pop(0)()
         lax.fori_loop(0, col_blocks, second_filter(stream), 0)
-
-    b_events(1)
-    for b in range(sequences):
-        taken = d1_buf[2 * b : 2 * b + 2].reshape(2 * runs, channels)
-        product = jnp.dot(taken, weights[1], preferred_element_type=jnp.float32)
-        level_rows = x1_buf[2 * b : 2 * b + 2, j, margin : margin + runs, :]
-        level_rows = level_rows.reshape(2 * runs, width)
-        mixed = (level_rows.astype(jnp.float32) + product).astype(jnp.bfloat16)
-        out_ref[b] = jnp.maximum(mixed[:runs], mixed[runs:])
-
-    swap.wait_send()
+    for event in rest:
+        event()
+
+    def out_copy(b, incoming):
+        return remote(
+            stage.at[other, b],
+            out_ref.at[(other if incoming else j) * mine + b],
+            out_send.at[b],
+            out_recv.at[b],
+            (other, q),
+        )
+
+    pairs_in(1)
+    for b in range(mine):
+        for h in range(2):
+            taken = d1_buf[2 * b : 2 * b + 2].reshape(2 * runs, channels)
+            product = jnp.dot(taken, weights[1, h], preferred_element_type=jnp.float32)
+            level_rows = x1_buf[
+                2 * b : 2 * b + 2, margin : margin + runs, h * width : (h + 1) * width
+            ].reshape(2 * runs, width)
+            mixed = (level_rows.astype(jnp.float32) + product).astype(jnp.bfloat16)
+            stage[h, b] = jnp.maximum(mixed[:runs], mixed[runs:])
+        out_copy(b, False).start()
+        out_ref[j * mine + b] = stage[j, b]
+
+    for b in range(mine):
+        out_copy(b, True).wait_recv()
+        out_copy(b, False).wait_send()
+    for copy in swap:
+        copy.wait_send()
     to_right.wait_send()
     to_left.wait_send()
     share.wait_send()
-    for stream in range(2 * sequences):
-        half_copy(stream, False).wait_send()
     sends_done(0)
     sends_done(1)
 
@@ -506,54 +584,56 @@
 def fused(bases, stem_weight, gains, depth_taps, point_weight):
     n_seq = lax.axis_size("seq")
     sequences, width_rows = bases.shape
-    taps, kinds, channels = stem_weight.shape
+    channels = stem_weight.shape[2]
     runs = width_rows // GROUP
     rows = runs + BLOCK
-    streams = sequences * GROUP
-    ids = bases.reshape(sequences, runs, GROUP).transpose(0, 2, 1).reshape(streams, runs)
-    stem = jnp.pad(stem_weight.reshape(taps * kinds, channels), ((0, 128 - taps * kinds), (0, 0)))
-    params = jnp.concatenate([gains, depth_taps[0]], axis=0).astype(jnp.float32)
-    params = jnp.pad(params, ((0, 8 - params.shape[0]), (0, 0)))
+    streams = sequences // 2 * GROUP
     half = channels // 2
     n_z = n_seq // 4
     slots = 4 * n_z - 1
     vmem = pl.BlockSpec(memory_space=pltpu.VMEM)
     dma = pltpu.SemaphoreType.DMA
     return pl.pallas_call(
-        functools.partial(encoder_kernel, n_seq, runs, taps),
+        functools.partial(encoder_kernel, n_seq),
         out_shape=jax.ShapeDtypeStruct((sequences, runs, half), jnp.bfloat16),
-        in_specs=[vmem] * 4,
+        in_specs=[vmem] * 5,
         out_specs=vmem,
         scratch_shapes=[
-            pltpu.VMEM((3, streams, runs), jnp.int32),
+            pltpu.VMEM((sequences, width_rows + 256), jnp.int32),
             pltpu.VMEM((2, 8, channels), jnp.float32),
-            pltpu.VMEM((128, 2 * runs), jnp.float32),
+            pltpu.VMEM((128, channels), jnp.float32),
+            pltpu.VMEM((128, channels), jnp.bfloat16),
+            pltpu.VMEM((128, width_rows + 128), jnp.float32),
+            pltpu.VMEM((width_rows + 128, 128), jnp.float32),
             pltpu.VMEM((streams, rows, 128), jnp.bfloat16),
             pltpu.VMEM((streams, rows, channels), jnp.bfloat16),
             pltpu.VMEM((streams, rows, channels), jnp.float32),
             pltpu.VMEM((streams, rows, channels), jnp.bfloat16),
-            pltpu.VMEM((streams // 2, 2, rows, half), jnp.bfloat16),
+            pltpu.VMEM((streams // 2, rows, channels), jnp.bfloat16),
             pltpu.VMEM((streams // 2, runs, channels), jnp.bfloat16),
-            pltpu.VMEM((2, channels, half), jnp.bfloat16),
+            pltpu.VMEM((2, 2, channels, half), jnp.bfloat16),
+            pltpu.VMEM((2, sequences // 2, runs, half), jnp.bfloat16),
             dma((2, slots)),
             dma((2, slots)),
-            dma((4,)),
-            dma((4,)),
+            dma((2, slots)),
+            dma((2, slots)),
+            dma((5,)),
+            dma((5,)),
             dma((3,)),
-            dma((streams // 2,)),
-            dma((streams // 2,)),
+            dma((sequences // 2,)),
+            dma((sequences // 2,)),
         ],
         compiler_params=pltpu.CompilerParams(
             collective_id=0, has_side_effects=True, vmem_limit_bytes=56 * 1024 * 1024
         ),
-    )(ids, stem, params, point_weight)
+    )(bases, stem_weight, gains, depth_taps, point_weight)
 
 
 def chosen(bases, stem_weight, gains, depth_taps, point_weight):
     n_seq = lax.axis_size("seq")
     taps, kinds, channels = stem_weight.shape
     fits = lax.axis_size("section") == 2 and n_seq % 4 == 0 and depth_taps.shape[1] == 5
-    fits = fits and bases.shape[1] == GROUP * 128 and (bases.shape[0] * GROUP) % 8 == 0
+    fits = fits and bases.shape[1] == GROUP * 128 and bases.shape[0] % 2 == 0
     fits = fits and channels % 256 == 0 and point_weight.shape[1] % BLOCK == 0
     fits = fits and kinds == 4 and taps * kinds <= 128
     run = fused if fits else shards

time: 74.9 us -> 61.6 us (0.82)
  the two profiles are of different devices: /device:TPU:12 before, /device:TPU:9 now
where the time goes in v2:
time: 61.6 us; the launch traced here: 61.4 us
  Pallas kernels  59.6 us (97%)
  local copies, waits for them, and re-layouts  1.77 us (3%)
    pallas_call x1, Pallas kernels, fused(): pl.pallas_call(functools.partial(encoder_kernel, n_seq), out_shape=jax.Sh...  59.6 us
    unnamed x1, local copies, waits for them, and re-layouts  1.77 us

profile of v2, /device:TPU:9, one launch (start us, length us, event | category | flops | bytes accessed | tf_op | source)
XLA Modules:
  0.0 61.4 jit_solution(5184944774136631423)
XLA Ops:
  0.0 59.6 %shard_map.55 = bf16[2,128,768]{2,1,0:T(8,128)(2,1)} custom-call(s32[2,512]{1,0:T(2,128)} %bases_ref.1, bf16[15,4,1536]{2,1,0:T(4,128)(2,1)} %stem_ref.1, bf16[1,1536]{1,0:T(2,128)(2,1)} %gains_ref.1, bf16[1,5,1536]{2,1,0:T(8,128)(2,1)} %taps_ref.1, bf16[1,96,1536]{2,1,0:T(8,128)(2,1)} %weight_ref.1), custom_call_target="tpu_custom_call" | custom-call | tf_op jit(solution)/shard_map/pallas_call | solution.py:596
  59.7 1.8 %copy.7 = bf16[2,128,768]{2,1,0:T(8,128)(2,1)} copy(bf16[2,128,768]{2,1,0:T(8,128)(2,1)} %shard_map.55) | data formatting | bytes 786432

commit v3 on v2

--- a/solution.py
+++ b/solution.py
@@ -399,7 +399,6 @@
             pair(level, slot).wait_send()
 
     own(0)
-    own(1)
     swap[1].start()
 
     stem_wide[...] = jnp.zeros_like(stem_wide)
@@ -491,7 +490,7 @@
 
     b_early = [[later(b_event, level, o, False) for o in range(n_z)] for level in range(2)]
     b_late = [[later(b_event, level, o, True) for o in range(n_z)] for level in range(2)]
-    interleaved(mine * GROUP * blocks, first_block, z_events[0] + a_events[0])
+    interleaved(mine * GROUP * blocks, first_block, z_events[0] + [later(own, 1)] + a_events[0])
     interleaved(
         mine * 2 * col_blocks, first_filter, z_events[1] + b_early[0] + a_events[1] + b_late[0]
     )
@@ -549,7 +548,7 @@
 
     def out_copy(b, incoming):
         return remote(
-            stage.at[other, b],
+            stage.at[b],
             out_ref.at[(other if incoming else j) * mine + b],
             out_send.at[b],
             out_recv.at[b],
@@ -558,16 +557,19 @@
 
     pairs_in(1)
     for b in range(mine):
-        for h in range(2):
+        for h in (other, j):
+            half = pl.ds(pl.multiple_of(h * width, 128), width)
             taken = d1_buf[2 * b : 2 * b + 2].reshape(2 * runs, channels)
             product = jnp.dot(taken, weights[1, h], preferred_element_type=jnp.float32)
-            level_rows = x1_buf[
-                2 * b : 2 * b + 2, margin : margin + runs, h * width : (h + 1) * width
-            ].reshape(2 * runs, width)
+            level_rows = x1_buf[2 * b : 2 * b + 2, margin : margin + runs, half]
+            level_rows = level_rows.reshape(2 * runs, width)
             mixed = (level_rows.astype(jnp.float32) + product).astype(jnp.bfloat16)
-            stage[h, b] = jnp.maximum(mixed[:runs], mixed[runs:])
-        out_copy(b, False).start()
-        out_ref[j * mine + b] = stage[j, b]
+            pooled = jnp.maximum(mixed[:runs], mixed[runs:])
+            if h is other:
+                stage[b] = pooled
+                out_copy(b, False).start()
+            else:
+                out_ref[j * mine + b] = pooled
 
     for b in range(mine):
         out_copy(b, True).wait_recv()
@@ -612,7 +614,7 @@
             pltpu.VMEM((streams // 2, rows, channels), jnp.bfloat16),
             pltpu.VMEM((streams // 2, runs, channels), jnp.bfloat16),
             pltpu.VMEM((2, 2, channels, half), jnp.bfloat16),
-            pltpu.VMEM((2, sequences // 2, runs, half), jnp.bfloat16),
+            pltpu.VMEM((sequences // 2, runs, half), jnp.bfloat16),
             dma((2, slots)),
             dma((2, slots)),
             dma((2, slots)),

time: 61.6 us -> 60.1 us (0.976)
  the two profiles are of different devices: /device:TPU:9 before, /device:TPU:0 now
where the time goes in v3:
time: 60.1 us; the launch traced here: 59.4 us
  Pallas kernels  57.6 us (96%)
  local copies, waits for them, and re-layouts  1.77 us (3%)
    pallas_call x1, Pallas kernels, fused(): pl.pallas_call(functools.partial(encoder_kernel, n_seq), out_shape=jax.Sh...  57.6 us
    unnamed x1, local copies, waits for them, and re-layouts  1.77 us

profile of v3, /device:TPU:0, one launch (start us, length us, event | category | flops | bytes accessed | tf_op | source)
XLA Modules:
  0.0 59.4 jit_solution(13789358271016158994)
XLA Ops:
  0.0 57.6 %shard_map.55 = bf16[2,128,768]{2,1,0:T(8,128)(2,1)} custom-call(s32[2,512]{1,0:T(2,128)} %bases_ref.1, bf16[15,4,1536]{2,1,0:T(4,128)(2,1)} %stem_ref.1, bf16[1,1536]{1,0:T(2,128)(2,1)} %gains_ref.1, bf16[1,5,1536]{2,1,0:T(8,128)(2,1)} %taps_ref.1, bf16[1,96,1536]{2,1,0:T(8,128)(2,1)} %weight_ref.1), custom_call_target="tpu_custom_call" | custom-call | tf_op jit(solution)/shard_map/pallas_call | solution.py:598
  57.6 1.8 %copy.7 = bf16[2,128,768]{2,1,0:T(8,128)(2,1)} copy(bf16[2,128,768]{2,1,0:T(8,128)(2,1)} %shard_map.55) | data formatting | bytes 786432
